TPU v7x, 128 devices: a whole 4x4x4 slice. The times are simulated.
128 devices in a mesh: dp: 16 (over z, y), section: 8 (over x, core).
Axes of the slice: x: 4, y: 4, z: 4, core: 2. Of those that a mesh axis runs over, the one named last changes fastest.
Arguments:
- queries: bfloat16 [8, 98304, 128], P(None, ('dp', 'section')), may hold values from -6 to 6
- grad_out: bfloat16 [8, 98304, 128], P(None, ('dp', 'section')), may hold values from -24 to 24
- log_norm: bfloat16 [8, 98304], P(None, ('dp', 'section')), may hold values from 2 to 10
- row_delta: bfloat16 [8, 98304], P(None, ('dp', 'section')), may hold values from -24 to 24
- key_rows: bfloat16 [98304, 128], P(('dp', 'section')), may hold values from -6 to 6
- value_rows: bfloat16 [98304, 128], P(('dp', 'section')), may hold values from -6 to 6
- doc_lengths: int32 [256], replicated, may hold values from 1 to 3072, as said below
Outputs:
- query_grad: bfloat16 [8, 98304, 128], P(None, ('dp', 'section'))
- key_grad: bfloat16 [98304, 128], P(('dp', 'section'))
- value_grad: bfloat16 [98304, 128], P(('dp', 'section'))
Inputs may be any that keep to these rules, and one draw needn't show every extreme that they name: `doc_lengths`: 256 document lengths in packing order that sum to 98304; the longest is exactly 3072.
All inputs are finite; a program needn't handle non-finite values.
Results may differ from a plain program's by a relative error of at most 0.0012.
The roundings to bfloat16 on the way count: a program that leaves them out, or rounds other values in their place, can miss the bound.
Values may be sent and summed in bfloat16 or wider, within the bound.
A program may use at most 192 MiB of HBM per device.

v0:
```python
import functools
import math

import jax
import jax.numpy as jnp
from jax import lax
from jax.experimental import pallas as pl
from jax.experimental.pallas import tpu as pltpu
from jax.sharding import PartitionSpec as P

AXES = ("dp", "section")
REACH = 4
CHUNK = 256
DIGIT = 16
STEPS = 14.0
MASKED = 32768.0
LOG2E = 1.4426950408889634
MESH = pl.DeviceIdType.MESH

NN = (((1,), (0,)), ((), ()))
NT = (((1,), (1,)), ((), ()))
dot = functools.partial(lax.dot_general, preferred_element_type=jnp.float32)

ORDER = (
    ((0, 2), (("kv", 1, 0),)),
    ((1, 0), (("kv", 1, 1),)),
    ((1, 1), (("kv", 1, 2), ("kv", 2, 0),)),
    ((2, 0), (("kv", 2, 1), ("kv", 2, 2),)),
    ((2, 2), (("kv", 3, 0), ("kv", 3, 1),)),
    ((3, 1), (("kv", 3, 2), ("kv", 4, 0),)),
    ((4, 0), (("kv", 4, 1),)),
    ((4, 1), (("kv", 4, 2), ("ret", 4, 0),)),
    ((4, 2), (("ret", 4, 1),)),
    ((3, 0), (("ret", 4, 2),)),
    ((3, 2), (("ret", 3, 1), ("ret", 3, 0),)),
    ((2, 1), (("ret", 3, 2),)),
    ((1, 2), (("ret", 2, 1), ("ret", 2, 0),)),
    ((0, 1), (("ret", 2, 2),)),
    ((0, 0), (("ret", 1, 1), ("ret", 1, 0),)),
    (None, (("ret", 1, 2),)),
)


def rows_of(offset, chunk, rows):
    if offset == 0:
        return chunk * CHUNK, rows
    if offset == REACH:
        return 0, (chunk + 1) * CHUNK
    return 0, rows


def kernel(
    count, sections, scale,
    q_in, g_in, norm_in, delta_in, k_in, v_in, lens_in,
    dq_out, dk_out, dv_out,
    qa, ga, qt, gt, kv, ka, va, dq, part, code, got, probs, grads, stat, base, ends,
    q_sem, g_sem, own_sem, kv_send, kv_recv, part_send, part_recv,
):
    heads, rows, width = dq.shape
    chunks = rows // CHUNK
    f32, b16 = jnp.float32, jnp.bfloat16
    me = lax.axis_index("dp") * sections + lax.axis_index("section")
    right = lax.rem(me + 1, count)
    left = lax.rem(me + count - 1, count)
    right = (right // sections, lax.rem(right, sections))
    left = (left // sections, lax.rem(left, sections))

    def load_q(h):
        return pltpu.make_async_copy(q_in.at[h], qa.at[h, :, pl.ds(0, width)], q_sem.at[h])

    def load_g(h):
        return pltpu.make_async_copy(g_in.at[h], ga.at[h, :, pl.ds(0, width)], g_sem.at[h])

    own = [
        pltpu.make_async_copy(ref.at[pl.ds(chunk * CHUNK, CHUNK)], kv.at[0, chunk, j], own_sem.at[chunk, j])
        for chunk in range(chunks)
        for j, ref in enumerate((k_in, v_in))
    ]
    for copy in own:
        copy.start()

    def start_loads(h, carry):
        load_q(h).start()
        load_g(h).start()
        return carry

    lax.fori_loop(0, heads, start_loads, 0)

    barrier = pltpu.get_barrier_semaphore()
    has_left, has_right = me > 0, me < count - 1

    @pl.when(has_left)
    def _():
        pl.semaphore_signal(barrier, inc=1, device_id=left, device_id_type=MESH)

    @pl.when(has_right)
    def _():
        pl.semaphore_signal(barrier, inc=1, device_id=right, device_id_type=MESH)

    def pass_on(offset, chunk):
        return pltpu.make_async_remote_copy(
            src_ref=kv.at[offset, chunk],
            dst_ref=kv.at[offset + 1, chunk],
            send_sem=kv_send.at[offset, chunk],
            recv_sem=kv_recv.at[offset, chunk],
            device_id=right,
            device_id_type=MESH,
        )

    def hand_back(offset, chunk):
        return pltpu.make_async_remote_copy(
            src_ref=code.at[offset - 1, chunk],
            dst_ref=got.at[offset - 1, chunk],
            send_sem=part_send.at[offset - 1, chunk],
            recv_sem=part_recv.at[offset - 1, chunk],
            device_id=left,
            device_id_type=MESH,
        )

    for copy in own:
        copy.wait()
    pl.semaphore_wait(barrier, has_left.astype(jnp.int32) + has_right.astype(jnp.int32))

    @pl.when(has_right)
    def _():
        for chunk in range(chunks):
            pass_on(0, chunk).start()

    for offset in range(1, REACH + 1):

        @pl.when(me < offset)
        def _(offset=offset):
            kv[offset] = jnp.zeros_like(kv[offset])

    @pl.when(me == count - 1)
    def _():
        got[...] = jnp.zeros_like(got)


    line = lax.broadcasted_iota(jnp.int32, (256, 256), 0)
    lane = lax.broadcasted_iota(jnp.int32, (256, 256), 1)
    lens = lens_in[...].astype(f32)
    ends[...] = jnp.sum(jnp.where(lane <= line, lens, 0.0), axis=1, keepdims=True)
    row = lax.broadcasted_iota(jnp.int32, (width, rows), 0)
    rowf = row.astype(f32)
    place = lax.broadcasted_iota(jnp.int32, (1, rows), 1)

    def matches(offset):
        first = lax.rem(me + count - offset, count) * rows
        where = (first + place).astype(f32)
        number = jnp.sum(jnp.where(ends[...] <= where, 1.0, 0.0), axis=0, keepdims=True)
        high = jnp.floor(number * (1.0 / DIGIT))
        low = number - high * DIGIT + DIGIT
        return (rowf == high) | (rowf == low)

    def key_side(offset):
        blocked = jnp.where(matches(offset), 0.0, -MASKED)
        ones = jnp.where(row < 2 * DIGIT + 3, 1.0, 0.0)
        key_part = jnp.where(row < 2 * DIGIT, blocked, ones).astype(b16).T
        value_part = jnp.where(row < 1, 1.0, 0.0).astype(b16).T
        for chunk in range(chunks):
            ka[offset, chunk, :, width:] = key_part[chunk * CHUNK : (chunk + 1) * CHUNK]
            va[offset, chunk, :, width:] = value_part[chunk * CHUNK : (chunk + 1) * CHUNK]

    def take_keys(offset, chunk):
        ka[offset, chunk, :, :width] = kv[offset, chunk, 0]
        va[offset, chunk, :, :width] = kv[offset, chunk, 1]

    base[...] = jnp.where(matches(0), 1.0, 0.0)
    stat[0] = norm_in[...].astype(f32) * (-1.0 / scale)
    stat[1] = -delta_in[...].astype(f32)

    def prepare(h, carry):
        norm = stat[0, pl.ds(h, 1), :]
        high = norm.astype(b16).astype(f32)
        middle = (norm - high).astype(b16).astype(f32)
        low = norm - high - middle
        extra = jnp.where(
            row == 2 * DIGIT,
            high,
            jnp.where(row == 2 * DIGIT + 1, middle, jnp.where(row == 2 * DIGIT + 2, low, base[...])),
        )
        qa[h, :, width:] = extra.astype(b16).T
        ga[h, :, width:] = jnp.where(row == 0, stat[1, pl.ds(h, 1), :], 0.0).astype(b16).T
        load_q(h).wait()
        load_g(h).wait()
        qt[h] = qa[h, :, :width].T
        gt[h] = ga[h, :, :width].T
        dq[h] = jnp.zeros((rows, width), f32)
        return carry

    lax.fori_loop(0, heads, prepare, 0)
    for offset in range(REACH + 1):
        key_side(offset)
    for chunk in range(chunks):
        take_keys(0, chunk)
    part[...] = jnp.zeros_like(part)

    def first_half(offset, chunk, at, h, slot):
        low, high = rows_of(offset, chunk, rows)
        scores = dot(qa[h, low:high, :], ka[at], NT)
        if offset == 0:
            i = lax.broadcasted_iota(jnp.int32, scores.shape, 0)
            j = lax.broadcasted_iota(jnp.int32, scores.shape, 1)
            scores = jnp.where(j <= i, scores, -1e30)
        p = jnp.exp2(scores * (scale * LOG2E))
        ds = p * dot(ga[h, low:high, :], va[at], NT)
        probs[slot, low:high, :] = p.astype(b16)
        grads[slot, low:high, :] = ds.astype(b16)

    def second_half(offset, chunk, at, h, slot):
        low, high = rows_of(offset, chunk, rows)
        p = probs[slot, low:high, :]
        ds = grads[slot, low:high, :]
        part[at[0], at[1], 0] += dot(qt[h, :, low:high], ds, NN)
        part[at[0], at[1], 1] += dot(gt[h, :, low:high], p, NN)
        dq[h, low:high, :] += dot(ds, kv[at[0], at[1], 0], NN)

    def encode(slot, chunk, total):
        top = jnp.max(jnp.abs(total), axis=1, keepdims=True)
        power = jnp.ceil(jnp.log2(jnp.maximum(top, 1e-30)))
        steps = jnp.floor(total * jnp.exp2(STEPS - power) + 0.5)
        for j in range(2):
            code[slot, chunk, j * width : (j + 1) * width, :] = steps[j].astype(jnp.int32).astype(jnp.int16)
        side = lax.broadcasted_iota(jnp.int32, (16, CHUNK), 0)
        powers = jnp.where(side == 0, power[0], jnp.where(side == 1, power[1], 0.0))
        code[slot, chunk, 2 * width :, :] = powers.astype(jnp.int32).astype(jnp.int16)

    def decoded(slot, chunk):
        power = got[slot, chunk, 2 * width :, :].astype(jnp.int32).astype(f32)
        unit = jnp.exp2(power - STEPS)
        return jnp.stack([
            got[slot, chunk, j * width : (j + 1) * width, :].astype(jnp.int32).astype(f32) * unit[j : j + 1, :]
            for j in range(2)
        ])

    def act(event):
        name, offset, chunk = event
        if name == "kv":

            @pl.when(me >= offset)
            def _():
                pass_on(offset - 1, chunk).wait_recv()

            if offset < REACH:

                @pl.when((me >= offset) & has_right)
                def _():
                    pass_on(offset, chunk).start()

            take_keys(offset, chunk)
        else:

            @pl.when(me >= offset)
            def _():
                total = part[offset, chunk]
                if offset < REACH:

                    @pl.when(has_right)
                    def _():
                        hand_back(offset + 1, chunk).wait_recv()

                    total += decoded(offset, chunk)
                encode(offset - 1, chunk, total)
                hand_back(offset, chunk).start()

    def like(one, other):
        return rows_of(*one, rows) == rows_of(*other, rows) and (one[0] == 0) == (other[0] == 0)

    ready = False
    n = 0
    while ORDER[n][0] is not None:
        end = n + 1
        while ORDER[end][0] is not None and like(ORDER[n][0], ORDER[end][0]):
            end += 1
        item, run = ORDER[n][0], ORDER[n:end]
        digits = [o * chunks + c for (o, c), _ in run]
        if not ready:
            for event in run[0][1]:
                act(event)
            first_half(*item, item, 0, 0)
        events_done = not ready

        def body(k, carry, run=run, item=item, digits=tuple(digits), events_done=events_done):
            for i, (_, events) in enumerate(run):
                if events and not (i == 0 and events_done):

                    @pl.when(k == i)
                    def _(events=events):
                        for event in events:
                            act(event)

            code = sum(d * 16**i for i, d in enumerate(digits))
            now = lax.rem(lax.shift_right_logical(code, 4 * k), 16)
            code = sum(d * 16**i for i, d in enumerate(digits[1:] + digits[-1:]))
            later = lax.rem(lax.shift_right_logical(code, 4 * k), 16)
            now = (now // chunks, lax.rem(now, chunks))
            later = (later // chunks, lax.rem(later, chunks))
            if len(run) == 1:
                now = item
            for h in range(heads):
                if h < heads - 1:
                    first_half(*item, now, h + 1, (h + 1) % 2)
                elif len(run) > 1:
                    first_half(*item, later, 0, 0)
                second_half(*item, now, h, h % 2)
            return carry

        if len(run) == 1:
            body(0, 0)
        else:
            lax.fori_loop(0, len(run), body, 0)
        ready = False
        n = end
    for event in ORDER[n][1]:
        act(event)

    def finish(h, carry):
        dq_out[h] = (dq[h] * scale).astype(b16)
        return carry

    lax.fori_loop(0, heads, finish, 0)
    for chunk in range(chunks):
        keys = slice(chunk * CHUNK, (chunk + 1) * CHUNK)

        @pl.when(has_right)
        def _(chunk=chunk):
            hand_back(1, chunk).wait_recv()

        total = part[0, chunk] + decoded(0, chunk)
        dk_out[keys, :] = (total[0] * scale).T.astype(b16)
        dv_out[keys, :] = total[1].T.astype(b16)
    for offset in range(REACH):

        @pl.when((me >= offset) & has_right)
        def _(offset=offset):
            for chunk in range(chunks):
                pass_on(offset, chunk).wait_send()

        @pl.when(me >= offset + 1)
        def _(offset=offset):
            for chunk in range(chunks):
                hand_back(offset + 1, chunk).wait_send()


def per_device(count, sections, queries, grad_out, log_norm, row_delta, key_rows, value_rows, doc_lengths):
    heads, rows, width = queries.shape
    chunks = rows // CHUNK
    scale = 1.0 / math.sqrt(width)
    f32, b16 = jnp.float32, jnp.bfloat16
    vmem = pl.BlockSpec(memory_space=pltpu.VMEM)
    anywhere = pl.BlockSpec(memory_space=pl.ANY)
    dma = pltpu.SemaphoreType.DMA
    blocks = heads * rows * (REACH + 1 - 1) * rows
    return pl.pallas_call(
        functools.partial(kernel, count, sections, scale),
        out_shape=(
            jax.ShapeDtypeStruct((heads, rows, width), b16),
            jax.ShapeDtypeStruct((rows, width), b16),
            jax.ShapeDtypeStruct((rows, width), b16),
        ),
        in_specs=[anywhere, anywhere, vmem, vmem, anywhere, anywhere, vmem],
        out_specs=(vmem, vmem, vmem),
        scratch_shapes=[
            pltpu.VMEM((heads, rows, 2 * width), b16),
            pltpu.VMEM((heads, rows, 2 * width), b16),
            pltpu.VMEM((heads, width, rows), b16),
            pltpu.VMEM((heads, width, rows), b16),
            pltpu.VMEM((REACH + 1, chunks, 2, CHUNK, width), b16),
            pltpu.VMEM((REACH + 1, chunks, CHUNK, 2 * width), b16),
            pltpu.VMEM((REACH + 1, chunks, CHUNK, 2 * width), b16),
            pltpu.VMEM((heads, rows, width), f32),
            pltpu.VMEM((REACH + 1, chunks, 2, width, CHUNK), f32),
            pltpu.VMEM((REACH, chunks, 2 * width + 16, CHUNK), jnp.int16),
            pltpu.VMEM((REACH, chunks, 2 * width + 16, CHUNK), jnp.int16),
            pltpu.VMEM((2, rows, CHUNK), b16),
            pltpu.VMEM((2, rows, CHUNK), b16),
            pltpu.VMEM((2, heads, rows), f32),
            pltpu.VMEM((width, rows), f32),
            pltpu.VMEM((256, 1), f32),
            dma((heads,)),
            dma((heads,)),
            dma((chunks, 2)),
            dma((REACH, chunks)),
            dma((REACH, chunks)),
            dma((REACH, chunks)),
            dma((REACH, chunks)),
        ],
        compiler_params=pltpu.CompilerParams(
            collective_id=0, has_side_effects=True, vmem_limit_bytes=40 * 1024 * 1024
        ),
        cost_estimate=pl.CostEstimate(
            flops=10 * blocks * width, bytes_accessed=8 * heads * rows * width, transcendentals=blocks
        ),
        name="packed_attention_grads",
    )(queries, grad_out, log_norm, row_delta, key_rows, value_rows, doc_lengths.reshape(1, -1))


def solution(mesh):
    placed = (
        P(None, AXES, None),
        P(None, AXES, None),
        P(None, AXES),
        P(None, AXES),
        P(AXES, None),
        P(AXES, None),
        P(),
    )
    return jax.shard_map(
        functools.partial(per_device, mesh.size, mesh.shape["section"]),
        mesh=mesh,
        in_specs=placed,
        out_specs=(P(None, AXES, None), P(AXES, None), P(AXES, None)),
        check_vma=False,
    )
```

profile of v0, /device:TPU:31, one launch (start us, length us, event | category | flops | bytes accessed | tf_op | source)
XLA Modules:
  0.0 76.5 jit_solution(8855981268896875484)
XLA Ops:
  0.6 0.0 copy-start
  0.6 1.4 %copy-done = bf16[8,768,128]{2,1,0:T(8,128)(2,1)S(1)} copy-done((bf16[8,768,128]{2,1,0:T(8,128)(2,1)S(1)}, bf16[8,768,128]{2,1,0:T(8,128)(2,1)}, u32[]{:S(2)}) %copy-start) | copy-done | bytes 1572888
  2.0 0.0 copy-start.1
  2.0 1.4 %copy-done.1 = bf16[8,768,128]{2,1,0:T(8,128)(2,1)S(1)} copy-done((bf16[8,768,128]{2,1,0:T(8,128)(2,1)S(1)}, bf16[8,768,128]{2,1,0:T(8,128)(2,1)}, u32[]{:S(2)}) %copy-start.1) | copy-done | bytes 1572888
  3.5 0.0 copy-start.2
  3.5 0.9 %copy-done.2 = bf16[768,128]{1,0:T(8,128)(2,1)S(1)} copy-done((bf16[768,128]{1,0:T(8,128)(2,1)S(1)}, bf16[768,128]{1,0:T(8,128)(2,1)}, u32[]{:S(2)}) %copy-start.2) | copy-done | bytes 196632
  4.4 0.0 copy-start.3
  4.4 0.9 %copy-done.3 = bf16[768,128]{1,0:T(8,128)(2,1)S(1)} copy-done((bf16[768,128]{1,0:T(8,128)(2,1)S(1)}, bf16[768,128]{1,0:T(8,128)(2,1)}, u32[]{:S(2)}) %copy-start.3) | copy-done | bytes 196632
  5.3 0.0 copy-start.4
  5.3 0.7 copy-done.4
  6.0 0.0 copy-start.5
  6.0 0.7 copy-done.5
  6.7 0.0 copy-start.6
  6.7 0.7 copy-done.6
  7.4 66.6 %packed_attention_grads.1 = (bf16[8,768,128]{2,1,0:T(8,128)(2,1)S(1)}, bf16[768,128]{1,0:T(8,128)(2,1)S(1)}, bf16[768,128]{1,0:T(8,128)(2,1)S(1)}) custom-call(bf16[8,768,128]{2,1,0:T(8,128)(2,1)S(1)} %copy-done, bf16[8,768,128]{2,1,0:T(8,128)(2,1)S(1)} %copy-done.1, bf16[8,768]{1,0:T(8,128)(2,1)S(1)} %copy-done.4, bf16[8,768]{1,0:T(8,128)(2,1)S(1)} %copy-done.5, ...), custom_call_target="tpu_custom_call" | custom-call | flops 24159191040 | bytes 6291456 | tf_op jit(solution)/shard_map/packed_attention_grads/pallas_call | solution.py:355
  74.0 1.1 %copy.13 = bf16[8,768,128]{2,1,0:T(8,128)(2,1)} copy(bf16[8,768,128]{2,1,0:T(8,128)(2,1)S(1)} %get-tuple-element.6) | data formatting | bytes 3145728
  75.2 0.7 copy.14
  75.8 0.7 copy.15
Async XLA Ops:
  0.6 1.4 %copy-start = (bf16[8,768,128]{2,1,0:T(8,128)(2,1)S(1)}, bf16[8,768,128]{2,1,0:T(8,128)(2,1)}, u32[]{:S(2)}) copy-start(bf16[8,768,128]{2,1,0:T(8,128)(2,1)} %q_in.1) | copy-start | bytes 4718596
  2.0 1.4 %copy-start.1 = (bf16[8,768,128]{2,1,0:T(8,128)(2,1)S(1)}, bf16[8,768,128]{2,1,0:T(8,128)(2,1)}, u32[]{:S(2)}) copy-start(bf16[8,768,128]{2,1,0:T(8,128)(2,1)} %g_in.1) | copy-start | bytes 4718596
  3.5 0.9 %copy-start.2 = (bf16[768,128]{1,0:T(8,128)(2,1)S(1)}, bf16[768,128]{1,0:T(8,128)(2,1)}, u32[]{:S(2)}) copy-start(bf16[768,128]{1,0:T(8,128)(2,1)} %k_in.1) | copy-start | bytes 589828
  4.4 0.9 %copy-start.3 = (bf16[768,128]{1,0:T(8,128)(2,1)S(1)}, bf16[768,128]{1,0:T(8,128)(2,1)}, u32[]{:S(2)}) copy-start(bf16[768,128]{1,0:T(8,128)(2,1)} %v_in.1) | copy-start | bytes 589828
  5.3 0.7 copy-start.4
  6.0 0.7 copy-start.5
  6.7 0.7 copy-start.6
where the time goes:
time: 76.9 us; the launch traced here: 76.5 us
  Pallas kernels  66.6 us (87%)
  local copies, waits for them, and re-layouts  9.25 us (12%)
    pallas_call x1, Pallas kernels, per_device(): pl.pallas_call(functools.partial(kernel, count, sections, scale), out_sha...  66.6 us
    unnamed x17, local copies, waits for them, and re-layouts  9.25 us

commit v1 on v0

--- a/solution.py
+++ b/solution.py
@@ -54,7 +54,7 @@
     q_in, g_in, norm_in, delta_in, k_in, v_in, lens_in,
     dq_out, dk_out, dv_out,
     qa, ga, qt, gt, kv, ka, va, dq, part, code, got, probs, grads, stat, base, ends,
-    q_sem, g_sem, own_sem, kv_send, kv_recv, part_send, part_recv,
+    norm_buf, delta_buf, lens_buf, dq_buf, q_sem, g_sem, small_sem, own_sem, kv_send, kv_recv, part_send, part_recv,
 ):
     heads, rows, width = dq.shape
     chunks = rows // CHUNK
@@ -76,7 +76,11 @@
         for chunk in range(chunks)
         for j, ref in enumerate((k_in, v_in))
     ]
-    for copy in own:
+    small = [
+        pltpu.make_async_copy(source, target, small_sem.at[i])
+        for i, (source, target) in enumerate(((norm_in, norm_buf), (delta_in, delta_buf), (lens_in, lens_buf)))
+    ]
+    for copy in own + small:
         copy.start()
 
     def start_loads(h, carry):
@@ -139,7 +143,9 @@
 
     line = lax.broadcasted_iota(jnp.int32, (256, 256), 0)
     lane = lax.broadcasted_iota(jnp.int32, (256, 256), 1)
-    lens = lens_in[...].astype(f32)
+    for copy in small:
+        copy.wait()
+    lens = lens_buf[...].astype(f32)
     ends[...] = jnp.sum(jnp.where(lane <= line, lens, 0.0), axis=1, keepdims=True)
     row = lax.broadcasted_iota(jnp.int32, (width, rows), 0)
     rowf = row.astype(f32)
@@ -167,8 +173,8 @@
         va[offset, chunk, :, :width] = kv[offset, chunk, 1]
 
     base[...] = jnp.where(matches(0), 1.0, 0.0)
-    stat[0] = norm_in[...].astype(f32) * (-1.0 / scale)
-    stat[1] = -delta_in[...].astype(f32)
+    stat[0] = norm_buf[...].astype(f32) * (-1.0 / scale)
+    stat[1] = -delta_buf[...].astype(f32)
 
     def prepare(h, carry):
         norm = stat[0, pl.ds(h, 1), :]
@@ -315,8 +321,12 @@
     for event in ORDER[n][1]:
         act(event)
 
+    def store(h):
+        return pltpu.make_async_copy(dq_buf.at[h], dq_out.at[h], q_sem.at[h])
+
     def finish(h, carry):
-        dq_out[h] = (dq[h] * scale).astype(b16)
+        dq_buf[h] = (dq[h] * scale).astype(b16)
+        store(h).start()
         return carry
 
     lax.fori_loop(0, heads, finish, 0)
@@ -330,6 +340,11 @@
         total = part[0, chunk] + decoded(0, chunk)
         dk_out[keys, :] = (total[0] * scale).T.astype(b16)
         dv_out[keys, :] = total[1].T.astype(b16)
+    def stored(h, carry):
+        store(h).wait()
+        return carry
+
+    lax.fori_loop(0, heads, stored, 0)
     for offset in range(REACH):
 
         @pl.when((me >= offset) & has_right)
@@ -349,7 +364,6 @@
     scale = 1.0 / math.sqrt(width)
     f32, b16 = jnp.float32, jnp.bfloat16
     vmem = pl.BlockSpec(memory_space=pltpu.VMEM)
-    anywhere = pl.BlockSpec(memory_space=pl.ANY)
     dma = pltpu.SemaphoreType.DMA
     blocks = heads * rows * (REACH + 1 - 1) * rows
     return pl.pallas_call(
@@ -359,8 +373,8 @@
             jax.ShapeDtypeStruct((rows, width), b16),
             jax.ShapeDtypeStruct((rows, width), b16),
         ),
-        in_specs=[anywhere, anywhere, vmem, vmem, anywhere, anywhere, vmem],
-        out_specs=(vmem, vmem, vmem),
+        in_specs=[pl.BlockSpec(memory_space=pl.ANY)] * 7,
+        out_specs=(pl.BlockSpec(memory_space=pl.ANY), vmem, vmem),
         scratch_shapes=[
             pltpu.VMEM((heads, rows, 2 * width), b16),
             pltpu.VMEM((heads, rows, 2 * width), b16),
@@ -378,8 +392,13 @@
             pltpu.VMEM((2, heads, rows), f32),
             pltpu.VMEM((width, rows), f32),
             pltpu.VMEM((256, 1), f32),
+            pltpu.VMEM(log_norm.shape, b16),
+            pltpu.VMEM(row_delta.shape, b16),
+            pltpu.VMEM((1, doc_lengths.size), jnp.int32),
+            pltpu.VMEM((heads, rows, width), b16),
             dma((heads,)),
             dma((heads,)),
+            dma((3,)),
             dma((chunks, 2)),
             dma((REACH, chunks)),
             dma((REACH, chunks)),
@@ -387,7 +406,7 @@
             dma((REACH, chunks)),
         ],
         compiler_params=pltpu.CompilerParams(
-            collective_id=0, has_side_effects=True, vmem_limit_bytes=40 * 1024 * 1024
+            collective_id=0, has_side_effects=True, vmem_limit_bytes=56 * 1024 * 1024
         ),
         cost_estimate=pl.CostEstimate(
             flops=10 * blocks * width, bytes_accessed=8 * heads * rows * width, transcendentals=blocks

time: 76.9 us -> 71.4 us (0.928)
  local copies, waits for them, and re-layouts: 9.25 us -> 4.08 us
    unnamed x17 -> x7, local copies, waits for them, and re-layouts: 9.25 us -> 4.08 us
where the time goes in v1:
time: 71.4 us; the launch traced here: 71.2 us
  Pallas kernels  66.5 us (93%)
  local copies, waits for them, and re-layouts  4.08 us (6%)
    pallas_call x1, Pallas kernels, per_device(): pl.pallas_call(functools.partial(kernel, count, sections, scale), out_sha...  66.5 us
    unnamed x7, local copies, waits for them, and re-layouts  4.08 us

profile of v1, /device:TPU:31, one launch (start us, length us, event | category | flops | bytes accessed | tf_op | source)
XLA Modules:
  0.0 71.2 jit_solution(15391549905322437910)
XLA Ops:
  0.6 66.5 %packed_attention_grads.1 = (bf16[8,768,128]{2,1,0:T(8,128)(2,1)}, bf16[768,128]{1,0:T(8,128)(2,1)}, bf16[768,128]{1,0:T(8,128)(2,1)}) custom-call(bf16[8,768,128]{2,1,0:T(8,128)(2,1)} %q_in.1, bf16[8,768,128]{2,1,0:T(8,128)(2,1)} %g_in.1, bf16[8,768]{1,0:T(8,128)(2,1)} %norm_in.1, bf16[8,768]{1,0:T(8,128)(2,1)} %delta_in.1, bf16[768,128]{1,0:T(8,128)(2,1)} %k_in.1, ...), custom_call_target="tpu_custom_call" | custom-call | flops 24159191040 | bytes 6291456 | tf_op jit(solution)/shard_map/packed_attention_grads/pallas_call | solution.py:369
  67.1 0.0 copy-start.1
  67.1 0.0 copy-start
  67.1 2.7 %copy.13 = bf16[8,768,128]{2,1,0:T(8,128)(2,1)} copy(bf16[8,768,128]{2,1,0:T(8,128)(2,1)} %get-tuple-element.6) | data formatting | bytes 3145728
  69.9 0.0 copy-done.1
  69.9 0.7 copy.14
  70.5 0.0 copy-done
  70.5 0.7 copy.15
Async XLA Ops:
  67.1 2.7 %copy-start.1 = (bf16[768,128]{1,0:T(8,128)(2,1)S(1)}, bf16[768,128]{1,0:T(8,128)(2,1)}, u32[]{:S(2)}) copy-start(bf16[768,128]{1,0:T(8,128)(2,1)} %get-tuple-element.7) | copy-start | bytes 589828
  67.1 3.4 %copy-start = (bf16[768,128]{1,0:T(8,128)(2,1)S(1)}, bf16[768,128]{1,0:T(8,128)(2,1)}, u32[]{:S(2)}) copy-start(bf16[768,128]{1,0:T(8,128)(2,1)} %get-tuple-element.8) | copy-start | bytes 589828
